TPU v7x, 32 devices: a whole 2x2x4 slice. The times are simulated.
32 devices in a mesh: mp: 2 (over x), row: 16 (over z, y, core).
Axes of the slice: x: 2, y: 2, z: 4, core: 2. Of those that a mesh axis runs over, the one named last changes fastest.
Arguments:
- radial_funcs: bfloat16 [128, 1024], P('row'), may hold values from -6 to 6
- kernels: bfloat16 [80, 1024], P('mp'), parts along dimension 0, may hold values from -0.0010299683 to 0.0010299683
- wigner: float32 [40, 128], replicated, may hold values from -4 to 4
- sources: bfloat16 [64, 2048], P('mp', 'row'), parts along dimension 0, may hold values from -6 to 6
- wigner_slots: int32 [2048], P('row'), may hold values from 0 to 127
- owners: int32 [2048], P('row'), may hold values from 0 to 7, as said below
- degrees: int32 [128], P('row'), may hold values from 0 to 30
- frequencies: float32 [2048], P('row'), may hold values from 0.5 to 2
Outputs:
- response: float32 [64, 2048], P('mp', 'row'), parts along dimension 0
There are 2 independent parts, one for each index of `mp`. A program takes and returns all parts, laid end to end along the dimension named above; an argument that names none is the same for every part. Nothing has to cross between parts.
Inputs may be any that keep to these rules, and one draw needn't show every extreme that they name: Within each aligned block of 128 singlets, owners never falls and every value 0 to 7 occurs.
All inputs are finite; a program needn't handle non-finite values.
Results may differ from a plain program's by a relative error of at most 0.0055.
Values may be sent and summed in bfloat16 or wider, within the bound.
A program may use at most 128 MiB of HBM per device.

v0:
```python
import jax
import jax.numpy as jnp
from jax import lax
from jax.sharding import PartitionSpec as P


def lookup(wigner, slot_block):
    return jnp.take(wigner, slot_block, axis=1)


def project(source_block, slot_block, owner_block, wigner, mult_dev):
    angular = lookup(wigner, slot_block)
    member = (owner_block[:, None] == jnp.arange(mult_dev, dtype=jnp.int32)[None, :]).astype(
        jnp.float32
    )
    scaled = angular[:, None, :] * source_block.astype(jnp.float32)[None, :, :]
    return jnp.einsum("skj,ja->ska", scaled, member, precision=lax.Precision.HIGHEST)


def selection(near_deg, far_deg, num_degree):
    level = jnp.arange(num_degree, dtype=jnp.int32)[:, None, None]
    total_deg = near_deg[None, :, None] + far_deg[None, None, :]
    diff_deg = jnp.abs(near_deg[None, :, None] - far_deg[None, None, :])
    return (diff_deg <= level) & (level <= total_deg) & ((total_deg + level) % 2 == 0)


def local(radial_funcs, kernels, wigner, sources, wigner_slots, owners, degrees, frequencies):
    num_degree = kernels.shape[0]
    mult_dev = radial_funcs.shape[0]
    own_part = project(sources, wigner_slots, owners, wigner, mult_dev).astype(jnp.bfloat16)
    projected, deg_all = (
        lax.all_gather(own_part, "row", axis=2, tiled=True),
        lax.all_gather(degrees, "row", axis=0, tiled=True),
    )
    weighted = (
        radial_funcs.astype(jnp.float32)[None] * kernels.astype(jnp.float32)[:, None, :]
    ).astype(jnp.bfloat16)
    weighted = weighted.reshape(num_degree * mult_dev, radial_funcs.shape[1])
    fetched = lax.all_gather(radial_funcs, "row", axis=0, tiled=True)
    piece_rows = fetched.shape[0]
    integral = lax.dot_general(
        weighted, fetched, (((1,), (1,)), ((), ())), preferred_element_type=jnp.float32
    )
    integral = integral.reshape(num_degree, mult_dev, piece_rows)
    kept_block = jnp.where(
        selection(degrees, deg_all, num_degree), integral, jnp.float32(0.0)
    ).astype(jnp.bfloat16)
    coupled = jnp.einsum("sab,skb->ska", kept_block, projected, preferred_element_type=jnp.float32)
    angular = lookup(wigner, wigner_slots)
    member = (owners[None, :] == jnp.arange(mult_dev, dtype=jnp.int32)[:, None]).astype(jnp.float32)
    spread = jnp.einsum("ska,ai->ski", coupled, member, precision=lax.Precision.HIGHEST)
    return frequencies[None, :] * sources.astype(jnp.float32) + jnp.sum(
        angular[:, None, :] * spread, axis=0
    )


def solution(mesh):
    in_specs = (
        P("row", None),
        P("mp", None),
        P(),
        P("mp", "row"),
        P("row"),
        P("row"),
        P("row"),
        P("row"),
    )
    out_specs = P("mp", "row")
    return jax.shard_map(local, mesh=mesh, in_specs=in_specs, out_specs=out_specs, check_vma=False)
```

profile of v0, /device:TPU:0, one launch (start us, length us, event | category | flops | bytes accessed | tf_op | source)
XLA Modules:
  0.0 67.7 jit_solution(15264262395300003951)
XLA Ops:
  0.0 0.8 %copy.11 = f32[40,128]{0,1:T(8,128)S(1)} copy(f32[40,128]{1,0:T(8,128)} %param.12) | data formatting | bytes 40960 | tf_op args[2]
  0.8 0.7 compare_select_fusion
  1.5 0.6 gather_fusion
  2.1 0.7 compare_and_fusion
  2.8 0.1 select_bitcast_fusion
  2.9 0.1 copy.12
  2.9 0.7 %convert_element_type.23 = f32[32,128]{1,0:T(8,128)S(1)} convert(bf16[32,128]{1,0:T(8,128)(2,1)} %param.13) | non-fusion elementwise | flops 4096 | bytes 24576 | tf_op jit(solution)/shard_map/convert_element_type | solution.py:52
  3.7 2.1 %fusion.7 = bf16[40,32,8]{1,2,0:T(8,128)(2,1)S(1)} fusion(f32[32,128]{1,0:T(8,128)S(1)} %convert_element_type.23, f32[40,128]{1,0:T(8,128)S(1)} %copy.12, s32[128]{0:T(128)} %param.15), kind=kOutput, calls=%fused_computation.9 | convolution fusion | flops 15893504 | bytes 57856 | tf_op jit(solution)/shard_map/skj,ja->ska/dot_general | solution.py:17
  5.8 0.1 copy.13
  5.9 0.0 copy-start.6
  5.9 0.0 copy-start.3
  6.0 0.0 copy-start.1
  6.0 26.2 %all_gather.9 = bf16[40,32,128]{0,1,2:T(8,128)(2,1)S(1)} all-gather(bf16[40,32,8]{0,1,2:T(8,128)(2,1)S(1)} %copy.13), channel_id=1, replica_groups=mesh['mp'=2,'row'=16] {'row'}, dimensions={2}, use_global_device_ids=true | all-gather | bytes 348160 | tf_op jit(solution)/shard_map/all_gather | solution.py:32
  32.2 0.0 copy-start
  32.2 1.4 %copy.14 = bf16[40,32,128]{2,1,0:T(8,128)(2,1)S(1)} copy(bf16[40,32,128]{0,1,2:T(8,128)(2,1)S(1)} %all_gather.9) | data formatting | bytes 655360 | tf_op jit(solution)/shard_map/all_gather | solution.py:32
  33.6 0.0 copy-done.6
  33.6 0.6 dynamic-slice
  34.8 0.0 copy-done.3
  34.8 0.2 dynamic-update-slice
  35.1 6.8 %all-reduce = s32[128]{0:T(128)S(1)} all-reduce(s32[128]{0:T(128)S(1)} %dynamic-update-slice), channel_id=1, replica_groups=mesh['mp'=2,'row'=16] {'row'}, use_global_device_ids=true, to_apply=%add | all-reduce | flops 128 | bytes 1024
  41.8 0.1 subtract_abs_fusion
  41.9 0.0 copy-done.1
  41.9 23.5 %all_gather.11 = bf16[128,1024]{1,0:T(8,128)(2,1)S(1)} all-gather(bf16[8,1024]{1,0:T(8,128)(2,1)S(1)} %copy-done.1), channel_id=1, replica_groups=mesh['mp'=2,'row'=16] {'row'}, dimensions={0}, use_global_device_ids=true | all-gather | bytes 278528 | tf_op jit(solution)/shard_map/all_gather | solution.py:39
  65.5 0.0 copy-done
  65.5 0.0 copy-start.2
  65.5 0.0 copy-start.4
  65.5 0.8 %fusion.2 = f32[40,32,8]{1,2,0:T(8,128)S(1)} fusion(bf16[40,32,128]{2,1,0:T(8,128)(2,1)S(1)} %copy.14, f32[40,1024]{1,0:T(8,128)S(1)} %convert_element_type.26, f32[8,1024]{1,0:T(8,128)S(1)} %convert_element_type.25, bf16[128,1024]{1,0:T(8,128)(2,1)S(1)} %all_gather.11, s32[8,128]{1,0:T(8,128)S(1)} %get-tuple-element.7, s32[8,128]{1,0:T(8,128)S(1)} %get-tuple-element.6), kind=kOutput, calls=%fused_computation.6 | convolution fusion | flops 87941120 | bytes 835584 | tf_op jit(solution)/shard_map/sab,skb->ska/dot_general | solution.py:48
  66.3 0.0 copy-done.5
  66.3 0.7 %fusion = f32[32,128]{1,0:T(8,128)S(1)} fusion(f32[40,32,8]{1,2,0:T(8,128)S(1)} %fusion.2, f32[40,128]{1,0:T(8,128)S(1)} %copy.12, s32[128]{0:T(128)S(1)} %copy-done.5), kind=kOutput, calls=%fused_computation.3 | convolution fusion | flops 16053248 | bytes 78336 | tf_op jit(solution)/shard_map/ska,ai->ski/dot_general | solution.py:51
  67.1 0.0 copy-done.2
  67.1 0.0 copy-done.4
  67.1 0.6 multiply_add_fusion
  (5 shorter events, 0.0 us)
Async XLA Ops:
  5.9 27.7 %copy-start.6 = (u32[32]{0:T(128)S(1)}, u32[32]{0:T(128)}, u32[]{:S(2)}) copy-start(u32[32]{0:T(128)} %constant.32) | copy-start | bytes 388
  5.9 28.9 %copy-start.3 = (s32[8]{0:T(128)S(1)}, s32[8]{0:T(128)}, u32[]{:S(2)}) copy-start(s32[8]{0:T(128)} %param.16) | copy-start | bytes 100
  6.0 36.0 %copy-start.1 = (bf16[8,1024]{1,0:T(8,128)(2,1)S(1)}, bf16[8,1024]{1,0:T(8,128)(2,1)}, u32[]{:S(2)}) copy-start(bf16[8,1024]{1,0:T(8,128)(2,1)} %param.10) | copy-start | bytes 49156
  32.2 33.3 %copy-start = (bf16[40,1024]{1,0:T(8,128)(2,1)S(1)}, bf16[40,1024]{1,0:T(8,128)(2,1)}, u32[]{:S(2)}) copy-start(bf16[40,1024]{1,0:T(8,128)(2,1)} %param.11) | copy-start | bytes 245764
  65.5 0.9 %copy-start.5 = (s32[128]{0:T(128)S(1)}, s32[128]{0:T(128)}, u32[]{:S(2)}) copy-start(s32[128]{0:T(128)} %param.15) | copy-start | bytes 1540
  65.5 1.6 %copy-start.2 = (bf16[32,128]{1,0:T(8,128)(2,1)S(1)}, bf16[32,128]{1,0:T(8,128)(2,1)}, u32[]{:S(2)}) copy-start(bf16[32,128]{1,0:T(8,128)(2,1)} %param.13) | copy-start | bytes 24580
  65.5 1.6 %copy-start.4 = (f32[128]{0:T(128)S(1)}, f32[128]{0:T(128)}, u32[]{:S(2)}) copy-start(f32[128]{0:T(128)} %param.17) | copy-start | bytes 1540
where the time goes:
time: 68 us; the launch traced here: 67.7 us
  blocking collectives  56.5 us (83%)
  local copies, waits for them, and re-layouts  3.89 us (6%)
  matrix products  3.68 us (5%)
  other arithmetic  2.84 us (4%)
  between operations  0.79 us (1%)
    all_gather x1, blocking collectives, local(): lax.all_gather(own_part, 'row', axis=2, tiled=True)  26.2 us
    all_gather x1, blocking collectives, local(): fetched = lax.all_gather(radial_funcs, 'row', axis=0, tiled=True)  23.5 us
    unnamed x1, blocking collectives  6.75 us
    dot_general x1, matrix products, project(): jnp.einsum('skj,ja->ska', scaled, member, precision=lax.Precision.HIGHEST)  2.11 us
    unnamed x17, local copies, waits for them, and re-layouts  1.69 us

commit v1 on v0

--- a/solution.py
+++ b/solution.py
@@ -1,7 +1,28 @@
+import functools
 import jax
 import jax.numpy as jnp
 from jax import lax
 from jax.sharding import PartitionSpec as P
+
+
+def search_cards_all(local_block, ax_name, dim_k):
+    dev_count = lax.axis_size(ax_name)
+    column = [(d, (d + 1) % dev_count) for d in range(dev_count)]
+    line_up = [(d, (d - 1) % dev_count) for d in range(dev_count)]
+    known, kept_arr = ([local_block], [local_block])
+    for _ in range(dev_count // 2):
+        known.append(lax.ppermute(known[-1], ax_name, column))
+    for _ in tuple(range((dev_count - 1) // 2)):
+        kept_arr.append(lax.ppermute(kept_arr[-1], ax_name, line_up))
+    then = jnp.concatenate([*known[::-1], *kept_arr[1:]], axis=dim_k)
+    return jnp.roll(
+        then,
+        shift=(lax.axis_index(ax_name) - dev_count // 2) * local_block.shape[dim_k],
+        axis=dim_k,
+    )
+
+
+obtain_pairs_all = functools.partial(search_cards_all, ax_name="row", dim_k=0)
 
 
 def lookup(wigner, slot_block):
@@ -36,7 +57,7 @@
         radial_funcs.astype(jnp.float32)[None] * kernels.astype(jnp.float32)[:, None, :]
     ).astype(jnp.bfloat16)
     weighted = weighted.reshape(num_degree * mult_dev, radial_funcs.shape[1])
-    fetched = lax.all_gather(radial_funcs, "row", axis=0, tiled=True)
+    fetched = obtain_pairs_all(radial_funcs)
     piece_rows = fetched.shape[0]
     integral = lax.dot_general(
         weighted, fetched, (((1,), (1,)), ((), ())), preferred_element_type=jnp.float32

time: 68 us -> 82.2 us (1.21)
  starting transfers between devices: 0 us -> 25.7 us
  blocking collectives: 56.5 us -> 33.2 us
  waiting for transfers between devices: 0 us -> 9.59 us
  local copies, waits for them, and re-layouts: 3.89 us -> 5.26 us
    ppermute x0 -> x15, starting transfers between devices: none -> 25.7 us  [the longest x7 24.7 us: search_cards_all(): kept_arr.append(lax.ppermute(kept_arr[-1], ax_name, line_up))]
    all_gather x1 -> x0, blocking collectives: 23.5 us -> none  [local(): fetched = lax.all_gather(radial_funcs, 'row', axis=0, tiled=True)]
    ppermute x0 -> x15, waiting for transfers between devices: none -> 9.59 us  [the longest x8 7.65 us: search_cards_all(): known.append(lax.ppermute(known[-1], ax_name, column))]
    unnamed x1, blocking collectives: 6.75 us -> 12.1 us
    all_gather x1, blocking collectives: 26.2 us -> 21.1 us  [local(): lax.all_gather(own_part, 'row', axis=2, tiled=True)]
    unnamed x17 -> x43, local copies, waits for them, and re-layouts: 1.69 us -> 3.07 us
  transfers between devices with their start and end apart: 0 -> 15, of which waited for: 0 -> 7; matrix products, arithmetic and copies ran while one was open for 0% -> 12% of each run, Pallas kernels for 0% -> 0%
where the time goes in v1:
time: 82.2 us; the launch traced here: 81.9 us
  blocking collectives  33.2 us (40%)
  starting transfers between devices  25.7 us (31%)
  waiting for transfers between devices  9.59 us (12%)
  local copies, waits for them, and re-layouts  5.26 us (6%)
  matrix products  3.69 us (4%)
  other arithmetic  3.47 us (4%)
  between operations  1.03 us (1%)
    ppermute x7, starting transfers between devices, search_cards_all(): kept_arr.append(lax.ppermute(kept_arr[-1], ax_name, line_up))  24.7 us
    all_gather x1, blocking collectives, local(): lax.all_gather(own_part, 'row', axis=2, tiled=True)  21.1 us
    unnamed x1, blocking collectives  12.1 us
    ppermute x8, waiting for transfers between devices, search_cards_all(): known.append(lax.ppermute(known[-1], ax_name, column))  7.65 us
    unnamed x43, local copies, waits for them, and re-layouts  3.07 us
    dot_general x1, matrix products, project(): jnp.einsum('skj,ja->ska', scaled, member, precision=lax.Precision.HIGHEST)  2.11 us
    ppermute x7, waiting for transfers between devices, search_cards_all(): kept_arr.append(lax.ppermute(kept_arr[-1], ax_name, line_up))  1.94 us
  transfers between devices with their start and end apart: 15, of which 7 were waited for; matrix products, arithmetic and copies ran while one was open for 12% of the time, Pallas kernels for 0%

profile of v1, /device:TPU:0, one launch (start us, length us, event | category | flops | bytes accessed | tf_op | source)
XLA Modules:
  0.0 81.9 jit_solution(17248213298762119469)
XLA Ops:
  0.0 0.5 collective-permute-start
  0.5 5.0 %collective-permute-start.8 = (bf16[8,1024]{1,0:T(8,128)(2,1)}, bf16[8,1024]{1,0:T(8,128)(2,1)S(1)}, u32[]{:S(2)}, u32[]{:S(2)}) collective-permute-start(bf16[8,1024]{1,0:T(8,128)(2,1)} %param.10), channel_id=1, source_target_pairs={{0,15},{1,0},{2,1},{3,2},{4,3},{5,4},{6,5},{7,6},{8,7},{9,8},{10,9... | collective-permute-start | bytes 49160 | tf_op jit(solution)/shard_map/ppermute | solution.py:16
  5.4 1.6 %collective-permute-done = bf16[8,1024]{1,0:T(8,128)(2,1)S(1)} collective-permute-done((bf16[8,1024]{1,0:T(8,128)(2,1)}, bf16[8,1024]{1,0:T(8,128)(2,1)S(1)}, u32[]{:S(2)}, u32[]{:S(2)}) %collective-permute-start) | collective-permute-done | bytes 16416 | tf_op jit(solution)/shard_map/ppermute | solution.py:14
  7.1 0.7 compare_select_fusion
  7.7 5.2 %collective-permute-done.1 = bf16[8,1024]{1,0:T(8,128)(2,1)S(1)} collective-permute-done((bf16[8,1024]{1,0:T(8,128)(2,1)S(1)}, bf16[8,1024]{1,0:T(8,128)(2,1)S(1)}, u32[]{:S(2)}, u32[]{:S(2)}) %collective-permute-start.1) | collective-permute-done | bytes 16416 | tf_op jit(solution)/shard_map/ppermute | solution.py:14
  12.9 0.7 compare_and_fusion
  13.6 4.4 %collective-permute-start.9 = (bf16[8,1024]{1,0:T(8,128)(2,1)S(1)}, bf16[8,1024]{1,0:T(8,128)(2,1)S(1)}, u32[]{:S(2)}, u32[]{:S(2)}) collective-permute-start(bf16[8,1024]{1,0:T(8,128)(2,1)S(1)} %collective-permute-done.8), channel_id=1, source_target_pairs={{0,15},{1,0},{2,1},{3,2},{4,3},{5,4},{6,5},{7,6},{8,7},{9,8},{10,9... | collective-permute-start | bytes 49160 | tf_op jit(solution)/shard_map/ppermute | solution.py:16
  18.0 0.8 collective-permute-done.2
  18.8 0.8 %copy.11 = f32[40,128]{0,1:T(8,128)S(1)} copy(f32[40,128]{1,0:T(8,128)} %param.12) | data formatting | bytes 40960 | tf_op args[2]
  19.6 0.6 gather_fusion
  20.3 4.5 %collective-permute-start.10 = (bf16[8,1024]{1,0:T(8,128)(2,1)S(1)}, bf16[8,1024]{1,0:T(8,128)(2,1)S(1)}, u32[]{:S(2)}, u32[]{:S(2)}) collective-permute-start(bf16[8,1024]{1,0:T(8,128)(2,1)S(1)} %collective-permute-done.9), channel_id=1, source_target_pairs={{0,15},{1,0},{2,1},{3,2},{4,3},{5,4},{6,5},{7,6},{8,7},{9,8},{10,9... | collective-permute-start | bytes 49160 | tf_op jit(solution)/shard_map/ppermute | solution.py:16
  24.8 0.1 select_bitcast_fusion
  24.9 0.7 convert_element_type.23
  25.6 0.6 collective-permute-done.10
  26.2 4.4 %collective-permute-start.11 = (bf16[8,1024]{1,0:T(8,128)(2,1)S(1)}, bf16[8,1024]{1,0:T(8,128)(2,1)S(1)}, u32[]{:S(2)}, u32[]{:S(2)}) collective-permute-start(bf16[8,1024]{1,0:T(8,128)(2,1)S(1)} %collective-permute-done.10), channel_id=1, source_target_pairs={{0,15},{1,0},{2,1},{3,2},{4,3},{5,4},{6,5},{7,6},{8,7},{9,8},{10,9... | collective-permute-start | bytes 49160 | tf_op jit(solution)/shard_map/ppermute | solution.py:16
  30.6 2.1 %fusion.7 = bf16[40,32,8]{1,2,0:T(8,128)(2,1)S(1)} fusion(f32[32,128]{1,0:T(8,128)S(1)} %convert_element_type.23, f32[40,128]{1,0:T(8,128)S(1)} %copy.12, s32[128]{0:T(128)} %param.15), kind=kOutput, calls=%fused_computation.9 | convolution fusion | flops 15893504 | bytes 57856 | tf_op jit(solution)/shard_map/skj,ja->ska/dot_general | solution.py:38
  32.8 1.3 %dynamic-slice = u32[1]{0:T(128)} dynamic-slice(u32[32]{0:T(128)} %constant.61, u32[]{:T(128)S(6)} %add.55), dynamic_slice_sizes={1} | dynamic-slice | bytes 12
  34.7 0.9 %dynamic-update-slice = s32[128]{0:T(128)S(1)} dynamic-update-slice(s32[128]{0:T(128)S(1)} %lt.27, s32[8]{0:T(128)} %param.16, u32[]{:T(128)} %bitcast.2) | dynamic-update-slice | bytes 68
  35.5 12.1 %all-reduce = s32[128]{0:T(128)S(1)} all-reduce(s32[128]{0:T(128)S(1)} %dynamic-update-slice), channel_id=1, replica_groups=mesh['mp'=2,'row'=16] {'row'}, use_global_device_ids=true, to_apply=%add | all-reduce | flops 128 | bytes 1024
  47.6 0.5 collective-permute-start.6
  48.1 0.7 subtract_abs_fusion
  48.9 0.1 copy.13
  49.0 0.1 collective-permute-done.12
  49.1 4.4 %collective-permute-start.13 = (bf16[8,1024]{1,0:T(8,128)(2,1)S(1)}, bf16[8,1024]{1,0:T(8,128)(2,1)S(1)}, u32[]{:S(2)}, u32[]{:S(2)}) collective-permute-start(bf16[8,1024]{1,0:T(8,128)(2,1)S(1)} %collective-permute-done.12), channel_id=1, source_target_pairs={{0,15},{1,0},{2,1},{3,2},{4,3},{5,4},{6,5},{7,6},{8,7},{9,8},{10,9... | collective-permute-start | bytes 49160 | tf_op jit(solution)/shard_map/ppermute | solution.py:16
  53.5 0.1 collective-permute-done.6
  53.5 21.1 %all_gather.6 = bf16[40,32,128]{0,1,2:T(8,128)(2,1)S(1)} all-gather(bf16[40,32,8]{0,1,2:T(8,128)(2,1)S(1)} %copy.13), channel_id=1, replica_groups=mesh['mp'=2,'row'=16] {'row'}, dimensions={2}, use_global_device_ids=true | all-gather | bytes 348160 | tf_op jit(solution)/shard_map/all_gather | solution.py:53
  74.6 1.4 %copy.14 = bf16[40,32,128]{2,1,0:T(8,128)(2,1)S(1)} copy(bf16[40,32,128]{0,1,2:T(8,128)(2,1)S(1)} %all_gather.6) | data formatting | bytes 655360 | tf_op jit(solution)/shard_map/all_gather | solution.py:53
  76.1 2.0 %collective-permute-start.14 = (bf16[8,1024]{1,0:T(8,128)(2,1)S(1)}, bf16[8,1024]{1,0:T(8,128)(2,1)S(1)}, u32[]{:S(2)}, u32[]{:S(2)}) collective-permute-start(bf16[8,1024]{1,0:T(8,128)(2,1)S(1)} %collective-permute-done.13), channel_id=1, source_target_pairs={{0,15},{1,0},{2,1},{3,2},{4,3},{5,4},{6,5},{7,6},{8,7},{9,8},{10,9... | collective-permute-start | bytes 49160 | tf_op jit(solution)/shard_map/ppermute | solution.py:16
  78.2 1.3 %collective-permute-done.14 = bf16[8,1024]{1,0:T(8,128)(2,1)S(1)} collective-permute-done((bf16[8,1024]{1,0:T(8,128)(2,1)S(1)}, bf16[8,1024]{1,0:T(8,128)(2,1)S(1)}, u32[]{:S(2)}, u32[]{:S(2)}) %collective-permute-start.14) | collective-permute-done | bytes 16416 | tf_op jit(solution)/shard_map/ppermute | solution.py:16
  79.7 0.8 %fusion.2 = f32[40,32,8]{1,2,0:T(8,128)S(1)} fusion(bf16[40,32,128]{2,1,0:T(8,128)(2,1)S(1)} %copy.14, f32[40,1024]{1,0:T(8,128)S(1)} %convert_element_type.26, f32[8,1024]{1,0:T(8,128)S(1)} %get-tuple-element.7, bf16[256,1024]{1,0:T(8,128)(2,1)S(1)} %constant_dynamic-update-slice_fusion, s32[]{:T(128)S(6)} %select_n.32, s32[8,128]{1,0:T(8,128)S(1)} %get-tuple-element.9, ...), kind=kOutput, calls=%fused_computation.6 | convolution fusion | flops 87941120 | bytes 835588 | tf_op jit(solution)/shard_map/sab,skb->ska/dot_general | solution.py:69
  80.5 0.7 fusion
  81.3 0.6 multiply_add_fusion
  (61 shorter events, 0.3 us)
Async XLA Ops:
  0.0 7.1 %collective-permute-start = (bf16[8,1024]{1,0:T(8,128)(2,1)}, bf16[8,1024]{1,0:T(8,128)(2,1)S(1)}, u32[]{:S(2)}, u32[]{:S(2)}) collective-permute-start(bf16[8,1024]{1,0:T(8,128)(2,1)} %param.10), channel_id=1, source_target_pairs={{0,1},{1,2},{2,3},{3,4},{4,5},{5,6},{6,7},{7,8},{8,9},{9,10},{10,1... | collective-permute-start | bytes 49160 | tf_op jit(solution)/shard_map/ppermute | solution.py:14
  0.5 13.2 %collective-permute-start.8 = (bf16[8,1024]{1,0:T(8,128)(2,1)}, bf16[8,1024]{1,0:T(8,128)(2,1)S(1)}, u32[]{:S(2)}, u32[]{:S(2)}) collective-permute-start(bf16[8,1024]{1,0:T(8,128)(2,1)} %param.10), channel_id=1, source_target_pairs={{0,15},{1,0},{2,1},{3,2},{4,3},{5,4},{6,5},{7,6},{8,7},{9,8},{10,9... | collective-permute-start | bytes 49160 | tf_op jit(solution)/shard_map/ppermute | solution.py:16
  7.1 5.9 %collective-permute-start.1 = (bf16[8,1024]{1,0:T(8,128)(2,1)S(1)}, bf16[8,1024]{1,0:T(8,128)(2,1)S(1)}, u32[]{:S(2)}, u32[]{:S(2)}) collective-permute-start(bf16[8,1024]{1,0:T(8,128)(2,1)S(1)} %collective-permute-done), channel_id=1, source_target_pairs={{0,1},{1,2},{2,3},{3,4},{4,5},{5,6},{6,7},{7,8},{8,9},{9,10},{10,1... | collective-permute-start | bytes 49160 | tf_op jit(solution)/shard_map/ppermute | solution.py:14
  12.9 5.9 %collective-permute-start.2 = (bf16[8,1024]{1,0:T(8,128)(2,1)S(1)}, bf16[8,1024]{1,0:T(8,128)(2,1)S(1)}, u32[]{:S(2)}, u32[]{:S(2)}) collective-permute-start(bf16[8,1024]{1,0:T(8,128)(2,1)S(1)} %collective-permute-done.1), channel_id=1, source_target_pairs={{0,1},{1,2},{2,3},{3,4},{4,5},{5,6},{6,7},{7,8},{8,9},{9,10},{10,1... | collective-permute-start | bytes 49160 | tf_op jit(solution)/shard_map/ppermute | solution.py:14
  13.6 6.7 %collective-permute-start.9 = (bf16[8,1024]{1,0:T(8,128)(2,1)S(1)}, bf16[8,1024]{1,0:T(8,128)(2,1)S(1)}, u32[]{:S(2)}, u32[]{:S(2)}) collective-permute-start(bf16[8,1024]{1,0:T(8,128)(2,1)S(1)} %collective-permute-done.8), channel_id=1, source_target_pairs={{0,15},{1,0},{2,1},{3,2},{4,3},{5,4},{6,5},{7,6},{8,7},{9,8},{10,9... | collective-permute-start | bytes 49160 | tf_op jit(solution)/shard_map/ppermute | solution.py:16
  18.8 6.0 %collective-permute-start.3 = (bf16[8,1024]{1,0:T(8,128)(2,1)S(1)}, bf16[8,1024]{1,0:T(8,128)(2,1)S(1)}, u32[]{:S(2)}, u32[]{:S(2)}) collective-permute-start(bf16[8,1024]{1,0:T(8,128)(2,1)S(1)} %collective-permute-done.2), channel_id=1, source_target_pairs={{0,1},{1,2},{2,3},{3,4},{4,5},{5,6},{6,7},{7,8},{8,9},{9,10},{10,1... | collective-permute-start | bytes 49160 | tf_op jit(solution)/shard_map/ppermute | solution.py:14
  20.3 5.9 %collective-permute-start.10 = (bf16[8,1024]{1,0:T(8,128)(2,1)S(1)}, bf16[8,1024]{1,0:T(8,128)(2,1)S(1)}, u32[]{:S(2)}, u32[]{:S(2)}) collective-permute-start(bf16[8,1024]{1,0:T(8,128)(2,1)S(1)} %collective-permute-done.9), channel_id=1, source_target_pairs={{0,15},{1,0},{2,1},{3,2},{4,3},{5,4},{6,5},{7,6},{8,7},{9,8},{10,9... | collective-permute-start | bytes 49160 | tf_op jit(solution)/shard_map/ppermute | solution.py:16
  24.8 5.9 %collective-permute-start.4 = (bf16[8,1024]{1,0:T(8,128)(2,1)S(1)}, bf16[8,1024]{1,0:T(8,128)(2,1)S(1)}, u32[]{:S(2)}, u32[]{:S(2)}) collective-permute-start(bf16[8,1024]{1,0:T(8,128)(2,1)S(1)} %collective-permute-done.3), channel_id=1, source_target_pairs={{0,1},{1,2},{2,3},{3,4},{4,5},{5,6},{6,7},{7,8},{8,9},{9,10},{10,1... | collective-permute-start | bytes 49160 | tf_op jit(solution)/shard_map/ppermute | solution.py:14
  26.2 21.4 %collective-permute-start.11 = (bf16[8,1024]{1,0:T(8,128)(2,1)S(1)}, bf16[8,1024]{1,0:T(8,128)(2,1)S(1)}, u32[]{:S(2)}, u32[]{:S(2)}) collective-permute-start(bf16[8,1024]{1,0:T(8,128)(2,1)S(1)} %collective-permute-done.10), channel_id=1, source_target_pairs={{0,15},{1,0},{2,1},{3,2},{4,3},{5,4},{6,5},{7,6},{8,7},{9,8},{10,9... | collective-permute-start | bytes 49160 | tf_op jit(solution)/shard_map/ppermute | solution.py:16
  30.6 17.0 %collective-permute-start.5 = (bf16[8,1024]{1,0:T(8,128)(2,1)S(1)}, bf16[8,1024]{1,0:T(8,128)(2,1)S(1)}, u32[]{:S(2)}, u32[]{:S(2)}) collective-permute-start(bf16[8,1024]{1,0:T(8,128)(2,1)S(1)} %collective-permute-done.4), channel_id=1, source_target_pairs={{0,1},{1,2},{2,3},{3,4},{4,5},{5,6},{6,7},{7,8},{8,9},{9,10},{10,1... | collective-permute-start | bytes 49160 | tf_op jit(solution)/shard_map/ppermute | solution.py:14
  47.6 1.4 %collective-permute-start.12 = (bf16[8,1024]{1,0:T(8,128)(2,1)S(1)}, bf16[8,1024]{1,0:T(8,128)(2,1)S(1)}, u32[]{:S(2)}, u32[]{:S(2)}) collective-permute-start(bf16[8,1024]{1,0:T(8,128)(2,1)S(1)} %collective-permute-done.11), channel_id=1, source_target_pairs={{0,15},{1,0},{2,1},{3,2},{4,3},{5,4},{6,5},{7,6},{8,7},{9,8},{10,9... | collective-permute-start | bytes 49160 | tf_op jit(solution)/shard_map/ppermute | solution.py:16
  47.6 5.9 %collective-permute-start.6 = (bf16[8,1024]{1,0:T(8,128)(2,1)S(1)}, bf16[8,1024]{1,0:T(8,128)(2,1)S(1)}, u32[]{:S(2)}, u32[]{:S(2)}) collective-permute-start(bf16[8,1024]{1,0:T(8,128)(2,1)S(1)} %collective-permute-done.5), channel_id=1, source_target_pairs={{0,1},{1,2},{2,3},{3,4},{4,5},{5,6},{6,7},{7,8},{8,9},{9,10},{10,1... | collective-permute-start | bytes 49160 | tf_op jit(solution)/shard_map/ppermute | solution.py:14
  49.0 27.0 %copy-start = (bf16[40,1024]{1,0:T(8,128)(2,1)S(1)}, bf16[40,1024]{1,0:T(8,128)(2,1)}, u32[]{:S(2)}) copy-start(bf16[40,1024]{1,0:T(8,128)(2,1)} %param.11) | copy-start | bytes 245764
  49.1 27.0 %collective-permute-start.13 = (bf16[8,1024]{1,0:T(8,128)(2,1)S(1)}, bf16[8,1024]{1,0:T(8,128)(2,1)S(1)}, u32[]{:S(2)}, u32[]{:S(2)}) collective-permute-start(bf16[8,1024]{1,0:T(8,128)(2,1)S(1)} %collective-permute-done.12), channel_id=1, source_target_pairs={{0,15},{1,0},{2,1},{3,2},{4,3},{5,4},{6,5},{7,6},{8,7},{9,8},{10,9... | collective-permute-start | bytes 49160 | tf_op jit(solution)/shard_map/ppermute | solution.py:16
  53.5 24.5 %collective-permute-start.7 = (bf16[8,1024]{1,0:T(8,128)(2,1)S(1)}, bf16[8,1024]{1,0:T(8,128)(2,1)S(1)}, u32[]{:S(2)}, u32[]{:S(2)}) collective-permute-start(bf16[8,1024]{1,0:T(8,128)(2,1)S(1)} %collective-permute-done.6), channel_id=1, source_target_pairs={{0,1},{1,2},{2,3},{3,4},{4,5},{5,6},{6,7},{7,8},{8,9},{9,10},{10,1... | collective-permute-start | bytes 49160 | tf_op jit(solution)/shard_map/ppermute | solution.py:14
  74.6 3.5 %copy-start.1 = (bf16[8,1024]{1,0:T(8,128)(2,1)S(1)}, bf16[8,1024]{1,0:T(8,128)(2,1)}, u32[]{:S(2)}) copy-start(bf16[8,1024]{1,0:T(8,128)(2,1)} %param.10) | copy-start | bytes 49156
  76.1 3.4 %collective-permute-start.14 = (bf16[8,1024]{1,0:T(8,128)(2,1)S(1)}, bf16[8,1024]{1,0:T(8,128)(2,1)S(1)}, u32[]{:S(2)}, u32[]{:S(2)}) collective-permute-start(bf16[8,1024]{1,0:T(8,128)(2,1)S(1)} %collective-permute-done.13), channel_id=1, source_target_pairs={{0,15},{1,0},{2,1},{3,2},{4,3},{5,4},{6,5},{7,6},{8,7},{9,8},{10,9... | collective-permute-start | bytes 49160 | tf_op jit(solution)/shard_map/ppermute | solution.py:16
  79.6 0.9 %copy-start.4 = (s32[128]{0:T(128)S(1)}, s32[128]{0:T(128)}, u32[]{:S(2)}) copy-start(s32[128]{0:T(128)} %param.15) | copy-start | bytes 1540
  79.6 1.6 %copy-start.2 = (bf16[32,128]{1,0:T(8,128)(2,1)S(1)}, bf16[32,128]{1,0:T(8,128)(2,1)}, u32[]{:S(2)}) copy-start(bf16[32,128]{1,0:T(8,128)(2,1)} %param.13) | copy-start | bytes 24580
  79.7 1.6 %copy-start.3 = (f32[128]{0:T(128)S(1)}, f32[128]{0:T(128)}, u32[]{:S(2)}) copy-start(f32[128]{0:T(128)} %param.17) | copy-start | bytes 1540
